TPU v7x, 32 devices: a whole 2x2x4 slice. The times are simulated.
32 devices in a mesh: region: 2 (over x), grid: 16 (over z, y, core).
Axes of the slice: x: 2, y: 2, z: 4, core: 2. Of those that a mesh axis runs over, the one named last changes fastest.
Arguments:
- radar_subimages: bfloat16 [768, 4, 2, 128, 128], P(('region', 'grid')), parts along dimension 0, may hold values from -25 to 25, as said below
- owning_sector: int32 [768, 1], P(('region', 'grid')), parts along dimension 0, may hold values from 0 to 15; in each aligned block of 24 rows (0 to 23, 24 to 47, ...) at most 2 rows name the same one
- sector_down_start: int32 [768], P(('region', 'grid')), parts along dimension 0, may hold values from 0 to 3
- sector_across_start: int32 [768], P(('region', 'grid')), parts along dimension 0, may hold values from 0 to 7
Outputs:
- coherence: float32 [3, 4096, 256], P(None, ('region', 'grid')), parts along dimension 1
There are 2 independent parts, one for each index of `region`. A program takes and returns all parts, laid end to end along the dimension named above; each array names one. Nothing has to cross between parts.
Inputs may be any that keep to these rules, and one draw needn't show every extreme that they name: `owning_sector`: the blocks of one device name any one tile at most 2 times, and some device's blocks name a tile exactly 2 times. `radar_subimages`: speckled complex samples whose dates are partly correlated with one another.
All inputs are finite; a program needn't handle non-finite values.
Results may differ from a plain program's by a relative error of at most 0.0003.
Values may be sent and summed in bfloat16 or wider, within the bound.
A program may use at most 128 MiB of HBM per device.

v0:
```python
import jax
import jax.numpy as jnp
from jax import lax
from jax.sharding import PartitionSpec as P

SUBIMAGE_BOUND = 2
TILE_TALL_PARTS = 4
TILE_WIDE_PARTS = 8


EPSILON = 1e-06


def extended(cells, sides, width):
    for axis, dim in sides:
        count = lax.axis_size(axis)
        ends = count - 1
        head = lax.slice_in_dim(cells, 0, width, axis=dim)
        tail = lax.slice_in_dim(cells, cells.shape[dim] - width, cells.shape[dim], axis=dim)
        cells = jnp.concatenate(
            [
                lax.ppermute(tail, axis, [(i, (i + 1) % count) for i in range(ends)]),
                cells,
                lax.ppermute(head, axis, [((i + 1) % count, i) for i in range(ends)]),
            ],
            axis=dim,
        )
    return cells


def assemble(pieces, slot_ids):
    slot_total = TILE_TALL_PARTS * TILE_WIDE_PARTS
    one_hot = slot_ids[None, :] == jnp.arange(slot_total)[:, None]
    counts = jnp.sum(one_hot.astype(jnp.int32), axis=1)
    summed = jnp.einsum(
        "sk,kdpyx->sdpyx", one_hot.astype(jnp.bfloat16), pieces, preferred_element_type=jnp.float32
    )
    merged_image = summed / jnp.maximum(counts, 1).astype(jnp.float32)[:, None, None, None, None]
    date_items = pieces.shape[1]
    side = pieces.shape[3]
    merged_image = merged_image.reshape(TILE_TALL_PARTS, TILE_WIDE_PARTS, date_items, 2, side, side)
    return merged_image.transpose(2, 3, 0, 4, 1, 5).reshape(
        date_items, 2, TILE_TALL_PARTS * side, TILE_WIDE_PARTS * side
    )


def products(merged_image):
    real_part = merged_image[:, 0]
    imag_part = merged_image[:, 1]
    cross_re = real_part[:-1] * real_part[1:] + imag_part[:-1] * imag_part[1:]
    cross_im = imag_part[:-1] * real_part[1:] - real_part[:-1] * imag_part[1:]
    powers = real_part * real_part + imag_part * imag_part
    return jnp.concatenate([cross_re, cross_im, powers], 0)


def columns_pass(fields):
    col_total = fields.shape[2]
    col_index = jnp.arange(col_total)[:, None]
    out_index = jnp.arange(col_total // 4)[None, :]
    window_table = ((col_index >= 4 * out_index - 12) & (col_index <= 4 * out_index + 15)).astype(
        jnp.float32
    )
    return jnp.einsum("frc,cj->frj", fields, window_table, precision=lax.Precision.HIGHEST)


def rows_pass(padded):
    row_total = padded.shape[1] - 4
    out_index = jnp.arange(row_total // 4)[:, None]
    row_index = jnp.arange(row_total + 4)[None, :]
    window_table = ((row_index >= 4 * out_index + 1) & (row_index <= 4 * out_index + 7)).astype(
        jnp.float32
    )
    return jnp.einsum("ip,fpj->fij", window_table, padded, precision=lax.Precision.HIGHEST)


def local(radar_subimages, owning_sector, sector_down_start, sector_across_start):
    group_size = lax.axis_size("grid")
    subimage_amount = radar_subimages.shape[0]
    instant_amount = radar_subimages.shape[1]
    subimage_breadth = radar_subimages.shape[3]
    target = owning_sector[:, 0]
    subimage_placing = jnp.arange(subimage_amount)
    same_tile = target[:, None] == target[None, :]
    earlier = jnp.sum(
        (same_tile & (subimage_placing[None, :] < subimage_placing[:, None])).astype(jnp.int32),
        axis=1,
    )
    lane_index = target * SUBIMAGE_BOUND + earlier
    lane_count = group_size * SUBIMAGE_BOUND
    chosen = lane_index[None, :] == jnp.arange(lane_count)[:, None]
    used_entries = jnp.any(chosen, axis=1)
    received_entry = jnp.sum(jnp.where(chosen, subimage_placing[None, :], 0), axis=1)
    outgoing = jnp.where(
        used_entries[:, None, None, None, None],
        radar_subimages[received_entry],
        jnp.zeros((), radar_subimages.dtype),
    )
    slot_number = sector_down_start * TILE_WIDE_PARTS + sector_across_start
    lane_slot = jnp.where(used_entries, slot_number[received_entry], -1)
    outgoing = outgoing.reshape(
        group_size, SUBIMAGE_BOUND, instant_amount, 2, subimage_breadth, subimage_breadth
    )
    lane_slot = lane_slot.reshape(group_size, SUBIMAGE_BOUND)
    arrived, arrived_slot = (
        lax.all_to_all(outgoing, "grid", split_axis=0, concat_axis=0, tiled=True),
        lax.all_to_all(lane_slot, "grid", split_axis=0, concat_axis=0, tiled=True),
    )
    merged_image = assemble(
        arrived.reshape(lane_count, instant_amount, 2, subimage_breadth, subimage_breadth),
        arrived_slot.reshape(lane_count),
    )
    padded = extended(merged_image, (("grid", 2),), 2)
    box_sums = rows_pass(columns_pass(products(padded)))
    couple_tally_value = instant_amount - 1
    magnitude = jnp.sqrt(
        box_sums[:couple_tally_value] ** 2
        + box_sums[couple_tally_value : 2 * couple_tally_value] ** 2
    )
    scale_root = jnp.sqrt(
        box_sums[2 * couple_tally_value : 3 * couple_tally_value]
        * box_sums[2 * couple_tally_value + 1 :]
        + EPSILON
    )
    return magnitude / scale_root


def solution(mesh):
    in_specs = (
        P(("region", "grid"), None, None, None, None),
        P(("region", "grid"), None),
        P(("region", "grid")),
        P(("region", "grid")),
    )
    out_specs = P(None, ("region", "grid"), None)
    return jax.shard_map(local, mesh=mesh, in_specs=in_specs, out_specs=out_specs, check_vma=False)
```

profile of v0, /device:TPU:16, one launch (start us, length us, event | category | flops | bytes accessed | tf_op | source)
XLA Modules:
  0.0 315.1 jit_solution(1546340872760809485)
XLA Ops:
  0.0 0.9 convert_reduce_fusion.1
  1.8 0.7 multiply_add_fusion
  2.5 0.7 gather_fusion
  3.2 0.7 select_n.38
  3.9 6.2 %all-to-all-start = ((s32[16,1,2]{2,1,0:T(1,128)}), s32[16,1,2]{2,1,0:T(1,128)S(1)}, u32[]{:S(2)}, u32[]{:S(2)}) async-start(s32[16,1,2]{2,1,0:T(1,128)} %bitcast.3), calls=%async_computation | async-start | bytes 16384 | tf_op jit(solution)/shard_map/all_to_all | solution.py:106
  10.1 7.8 %gather_fusion.1 = bf16[32,4,2,128,128]{4,3,2,1,0:T(8,128)(2,1)} fusion(bf16[24,4,2,128,128]{4,3,2,1,0:T(8,128)(2,1)} %param.4, s32[1024]{0:T(1024)S(1)} %pad_clamp_fusion), kind=kCustom, calls=%fused_computation.1 | custom fusion | bytes 16777344 | tf_op jit(solution)/shard_map/gather | solution.py:95
  17.9 7.2 %broadcast_select_fusion = bf16[16,2,4,2,128,128]{5,4,3,2,1,0:T(8,128)(2,1)} fusion(bf16[16,2,4,2,128,128]{5,4,3,2,1,0:T(8,128)(2,1)} %bitcast.38, pred[16,2]{1,0:T(8,128)(4,1)S(1)} %broadcast_in_dim.47), kind=kLoop, calls=%fused_computation.15 | loop fusion | flops 4194304 | bytes 16777248 | tf_op jit(solution)/shard_map/jit(_where)/select_n | solution.py:93
  25.1 16.3 %copy.34 = bf16[16,2,4,2,128,128]{5,1,4,3,2,0:T(2,128)(2,1)} copy(bf16[16,2,4,2,128,128]{5,4,3,2,1,0:T(8,128)(2,1)} %broadcast_select_fusion) | data formatting | bytes 16777216 | tf_op jit(solution)/shard_map/jit(_where)/select_n | solution.py:93
  41.4 6.0 %all-to-all-start.1 = ((bf16[16,2,4,2,128,128]{5,1,4,3,2,0:T(2,128)(2,1)}), bf16[16,2,4,2,128,128]{5,1,4,3,2,0:T(2,128)(2,1)}, u32[]{:S(2)}, u32[]{:S(2)}) async-start(bf16[16,2,4,2,128,128]{5,1,4,3,2,0:T(2,128)(2,1)} %copy.34), calls=%async_computation.1 | async-start | bytes 16777216 | tf_op jit(solution)/shard_map/all_to_all | solution.py:105
  48.8 181.2 %all-to-all-done.1 = bf16[16,2,4,2,128,128]{5,1,4,3,2,0:T(2,128)(2,1)} async-done(((bf16[16,2,4,2,128,128]{5,1,4,3,2,0:T(2,128)(2,1)}), bf16[16,2,4,2,128,128]{5,1,4,3,2,0:T(2,128)(2,1)}, u32[]{:S(2)}, u32[]{:S(2)}) %all-to-all-start.1) | async-done | bytes 8388640 | tf_op jit(solution)/shard_map/all_to_all | solution.py:105
  230.0 7.4 %copy.35 = bf16[16,2,4,2,128,128]{5,1,0,4,3,2:T(2,128)(2,1)S(1)} copy(bf16[16,2,4,2,128,128]{5,1,4,3,2,0:T(2,128)(2,1)} %all-to-all-done.1) | data formatting | bytes 16777216 | tf_op jit(solution)/shard_map/all_to_all | solution.py:105
  237.4 2.3 divide_bitcast_fusion
  239.7 6.0 %copy.47 = f32[4,8,4,2,128,128]{5,1,4,0,3,2:T(8,128)} copy(f32[4,8,4,2,128,128]{5,1,0,4,3,2:T(8,128)S(1)} %divide_bitcast_fusion) | data formatting | bytes 33554432 | tf_op jit(solution)/shard_map/reshape | solution.py:41
  245.7 18.0 %reshape.101 = f32[4,2,512,1024]{3,2,1,0:T(8,128)} reshape(f32[4,2,4,128,8,128]{5,4,3,2,1,0:T(8,128)} %bitcast.37) | data formatting | bytes 33554432 | tf_op jit(solution)/shard_map/reshape | solution.py:42
  263.8 1.1 fusion.34
  264.8 1.9 collective-permute-start
  266.8 4.7 %collective-permute-start.1 = (f32[4,2,2,1024]{3,2,0,1:T(2,128)S(1)}, f32[4,2,2,1024]{3,2,0,1:T(2,128)S(1)}, u32[]{:S(2)}, u32[]{:S(2)}) collective-permute-start(f32[4,2,2,1024]{3,2,0,1:T(2,128)S(1)} %get-tuple-element.8), channel_id=1, source_target_pairs={{1,0},{2,1},{3,2},{4,3},{5,4},{6,5},{7,6},{8,7},{9,8},{10,9},{11,1... | collective-permute-start | bytes 196616 | tf_op jit(solution)/shard_map/ppermute | solution.py:24
  271.5 1.7 collective-permute-done.1
  273.2 7.1 %pad_maximum_fusion = f32[4,2,516,1024]{3,2,0,1:T(8,128)S(1)} fusion(f32[4,2,2,1024]{3,2,0,1:T(2,128)S(1)} %collective-permute-done.1, f32[4,2,2,1024]{3,2,0,1:T(2,128)S(1)} %collective-permute-done, f32[4,2,512,1024]{3,2,1,0:T(8,128)} %reshape.101), kind=kLoop, calls=%fused_computation.8 | loop fusion | flops 8454144 | bytes 33816576 | tf_op jit(solution)/shard_map/concatenate | solution.py:20
  280.3 6.2 %add_bitcast_fusion = (f32[3,516,1024]{2,1,0:T(8,128)}, f32[3,516,1024]{2,1,0:T(8,128)}) fusion(f32[4,2,516,1024]{3,2,0,1:T(8,128)S(1)} %pad_maximum_fusion), kind=kLoop, calls=%fused_computation.17 | loop fusion | flops 9510912 | bytes 38043648 | tf_op jit(solution)/shard_map/add | solution.py:50
  286.5 4.3 %fusion.7 = f32[4,516,1024]{2,1,0:T(8,128)} fusion(f32[4,2,516,1024]{3,2,0,1:T(8,128)S(1)} %pad_maximum_fusion), kind=kLoop, calls=%fused_computation.13 | loop fusion | flops 6340608 | bytes 25362432 | tf_op jit(solution)/shard_map/add | solution.py:52
  290.8 15.8 %fusion = f32[10,516,256]{2,1,0:T(8,128)} fusion(f32[4,516,1024]{2,1,0:T(8,128)} %fusion.7, f32[3,516,1024]{2,1,0:T(8,128)} %get-tuple-element.6, f32[3,516,1024]{2,1,0:T(8,128)} %get-tuple-element.5, s32[256]{0:T(256)S(1)} %get-tuple-element.9, s32[256]{0:T(256)S(1)} %get-tuple-element.10), kind=kOutput, calls=%fused_computation.2 | convolution fusion | flops 16243310592 | bytes 26421248 | tf_op jit(solution)/shard_map/frc,cj->frj/dot_general | solution.py:63
  306.6 7.4 %convolution_bitcast_fusion = f32[10,128,256]{1,2,0:T(8,128)S(1)} fusion(f32[10,516,256]{2,1,0:T(8,128)} %fusion, s32[128]{0:T(128)S(1)} %get-tuple-element.11, s32[128]{0:T(128)S(1)} %get-tuple-element.12), kind=kOutput, calls=%fused_computation.20 | convolution fusion | flops 2029192704 | bytes 6595584 | tf_op jit(solution)/shard_map/ip,fpj->fij/dot_general | solution.py:73
  314.2 0.9 copy.40
  (17 shorter events, 2.5 us)
Async XLA Ops:
  3.9 37.5 %all-to-all-start = ((s32[16,1,2]{2,1,0:T(1,128)}), s32[16,1,2]{2,1,0:T(1,128)S(1)}, u32[]{:S(2)}, u32[]{:S(2)}) async-start(s32[16,1,2]{2,1,0:T(1,128)} %bitcast.3), calls=%async_computation | async-start | bytes 16384 | tf_op jit(solution)/shard_map/all_to_all | solution.py:106
  41.4 188.6 %all-to-all-start.1 = ((bf16[16,2,4,2,128,128]{5,1,4,3,2,0:T(2,128)(2,1)}), bf16[16,2,4,2,128,128]{5,1,4,3,2,0:T(2,128)(2,1)}, u32[]{:S(2)}, u32[]{:S(2)}) async-start(bf16[16,2,4,2,128,128]{5,1,4,3,2,0:T(2,128)(2,1)} %copy.34), calls=%async_computation.1 | async-start | bytes 16777216 | tf_op jit(solution)/shard_map/all_to_all | solution.py:105
  264.8 6.7 %collective-permute-start = (f32[4,2,2,1024]{3,2,0,1:T(2,128)S(1)}, f32[4,2,2,1024]{3,2,0,1:T(2,128)S(1)}, u32[]{:S(2)}, u32[]{:S(2)}) collective-permute-start(f32[4,2,2,1024]{3,2,0,1:T(2,128)S(1)} %get-tuple-element.7), channel_id=1, source_target_pairs={{0,1},{1,2},{2,3},{3,4},{4,5},{5,6},{6,7},{7,8},{8,9},{9,10},{10,1... | collective-permute-start | bytes 196616 | tf_op jit(solution)/shard_map/ppermute | solution.py:22
  266.8 6.4 %collective-permute-start.1 = (f32[4,2,2,1024]{3,2,0,1:T(2,128)S(1)}, f32[4,2,2,1024]{3,2,0,1:T(2,128)S(1)}, u32[]{:S(2)}, u32[]{:S(2)}) collective-permute-start(f32[4,2,2,1024]{3,2,0,1:T(2,128)S(1)} %get-tuple-element.8), channel_id=1, source_target_pairs={{1,0},{2,1},{3,2},{4,3},{5,4},{6,5},{7,6},{8,7},{9,8},{10,9},{11,1... | collective-permute-start | bytes 196616 | tf_op jit(solution)/shard_map/ppermute | solution.py:24
where the time goes:
time: 318 us; the launch traced here: 315 us
  waiting for transfers between devices  183 us (58%)
  local copies, waits for them, and re-layouts  59.5 us (19%)
  other arithmetic  28.2 us (9%)
  matrix products  25.5 us (8%)
  starting transfers between devices  18.9 us (6%)
    all_to_all x1, waiting for transfers between devices, local(): lax.all_to_all(outgoing, 'grid', split_axis=0, concat_axis=0, tiled=True)  181 us
    reshape x1, local copies, waits for them, and re-layouts, assemble(): merged_image.transpose(2, 3, 0, 4, 1, 5)  18 us
    select_n x1, local copies, waits for them, and re-layouts, local(): jnp.where(used_entries[:, None, None, None, None], radar_subimages[receiv...  16.3 us
    dot_general x1, matrix products, columns_pass(): jnp.einsum('frc,cj->frj', fields, window_table, precision=lax.Precision.H...  15.8 us
    gather x1, local copies, waits for them, and re-layouts, local(): radar_subimages[received_entry]  7.76 us
    all_to_all x1, local copies, waits for them, and re-layouts, local(): lax.all_to_all(outgoing, 'grid', split_axis=0, concat_axis=0, tiled=True)  7.44 us
    dot_general x1, matrix products, rows_pass(): jnp.einsum('ip,fpj->fij', window_table, padded, precision=lax.Precision.H...  7.38 us
    select_n x1, other arithmetic, local(): jnp.where(used_entries[:, None, None, None, None], radar_subimages[receiv...  7.22 us
  transfers between devices with their start and end apart: 4, of which 2 were waited for; matrix products, arithmetic and copies ran while one was open for 10% of the time, Pallas kernels for 0%

commit v1 on v0

v1 whole, which is shorter than its diff:
```python
import functools

import jax
import jax.numpy as jnp
from jax import lax
from jax.experimental import pallas as pl
from jax.experimental.pallas import tpu as pltpu
from jax.sharding import PartitionSpec as P

SUBIMAGE_BOUND = 2
TILE_TALL_PARTS = 4
TILE_WIDE_PARTS = 8
LOOK = 4

EPSILON = 1e-06
MIB = 1 << 20
MESH = pl.DeviceIdType.MESH


def exchange_kernel(
    group,
    owner_ref,
    down_ref,
    across_ref,
    blocks_ref,
    arrived_ref,
    slots_ref,
    staged,
    notes,
    send_sem,
    recv_sem,
    note_send_sem,
    note_recv_sem,
    own_sem,
):
    me = lax.axis_index("grid")
    held = blocks_ref.shape[0]
    lane = lax.broadcasted_iota(jnp.int32, notes.shape[1:], 1)

    def stage(t):
        first, second = jnp.int32(0), jnp.int32(0)
        first_slot, second_slot = jnp.int32(-1), jnp.int32(-1)
        found = jnp.int32(0)
        for b in range(held):
            hit = owner_ref[b] == t
            slot = down_ref[b] * TILE_WIDE_PARTS + across_ref[b]
            take_first = jnp.logical_and(hit, found == 0)
            take_second = jnp.logical_and(hit, found != 0)
            first = jnp.where(take_first, b, first)
            first_slot = jnp.where(take_first, slot, first_slot)
            second = jnp.where(take_second, b, second)
            second_slot = jnp.where(take_second, slot, second_slot)
            found = jnp.where(hit, 1, found)
        staged[t, 0] = blocks_ref[first]
        staged[t, 1] = blocks_ref[second]
        notes[t] = jnp.where(lane == 0, first_slot, jnp.where(lane == 1, second_slot, -1))

    def copies(k):
        t = lax.rem(me + k, group)
        return (
            pltpu.make_async_remote_copy(
                src_ref=staged.at[t],
                dst_ref=arrived_ref.at[me],
                send_sem=send_sem.at[k],
                recv_sem=recv_sem.at[k],
                device_id={"grid": t},
                device_id_type=MESH,
            ),
            pltpu.make_async_remote_copy(
                src_ref=notes.at[t],
                dst_ref=slots_ref.at[me],
                send_sem=note_send_sem.at[k],
                recv_sem=note_recv_sem.at[k],
                device_id={"grid": t},
                device_id_type=MESH,
            ),
        )

    barrier = pltpu.get_barrier_semaphore()

    def greet(k, _):
        pl.semaphore_signal(
            barrier, inc=1, device_id={"grid": lax.rem(me + k, group)}, device_id_type=MESH
        )
        return 0

    lax.fori_loop(1, group, greet, 0)
    pl.semaphore_wait(barrier, group - 1)

    def send(k, _):
        stage(lax.rem(me + k, group))
        block, note = copies(k)
        block.start()
        note.start()
        return 0

    lax.fori_loop(1, group, send, 0)
    stage(me)
    own = (
        pltpu.make_async_copy(staged.at[me], arrived_ref.at[me], own_sem.at[0]),
        pltpu.make_async_copy(notes.at[me], slots_ref.at[me], own_sem.at[1]),
    )
    for copy in own:
        copy.start()

    def finish(k, _):
        for copy in copies(k):
            copy.wait()
        return 0

    lax.fori_loop(1, group, finish, 0)
    for copy in own:
        copy.wait()


def exchange(blocks, owner, down, across):
    group = lax.axis_size("grid")
    held, rows, side = blocks.shape
    staged_bytes = group * SUBIMAGE_BOUND * rows * side * 2
    return pl.pallas_call(
        functools.partial(exchange_kernel, group),
        out_shape=(
            jax.ShapeDtypeStruct((group, SUBIMAGE_BOUND, rows, side), blocks.dtype),
            jax.ShapeDtypeStruct((group, 8, side), jnp.int32),
        ),
        in_specs=[pl.BlockSpec(memory_space=pltpu.SMEM)] * 3
        + [pl.BlockSpec(memory_space=pltpu.VMEM)],
        out_specs=(pl.BlockSpec(memory_space=pl.ANY), pl.BlockSpec(memory_space=pl.ANY)),
        scratch_shapes=[
            pltpu.VMEM((group, SUBIMAGE_BOUND, rows, side), blocks.dtype),
            pltpu.VMEM((group, 8, side), jnp.int32),
            pltpu.SemaphoreType.DMA((group,)),
            pltpu.SemaphoreType.DMA((group,)),
            pltpu.SemaphoreType.DMA((group,)),
            pltpu.SemaphoreType.DMA((group,)),
            pltpu.SemaphoreType.DMA((2,)),
        ],
        compiler_params=pltpu.CompilerParams(
            collective_id=0,
            has_side_effects=True,
            vmem_limit_bytes=staged_bytes + held * rows * side * 2 + 6 * MIB,
        ),
    )(owner, down, across, blocks)


def split_dot(values, table):
    total = None
    rest = values
    for _ in range(3):
        part = rest.astype(jnp.bfloat16)
        rest = rest - part.astype(jnp.float32)
        term = jnp.dot(part, table, preferred_element_type=jnp.float32)
        total = term if total is None else total + term
    return total


def looks_kernel(
    dates, side, slots_ref, arrived_ref, box_ref, edge_ref, image, mid, up, low, edges, table, head, following, amount
):
    slot_total = TILE_TALL_PARTS * TILE_WIDE_PARTS
    lanes = arrived_ref.shape[0]
    channels = 2 * dates
    pairs = dates - 1
    fields = 2 * pairs + dates
    width = TILE_WIDE_PARTS * side
    looks_down = side // LOOK
    rows_out = TILE_TALL_PARTS * looks_down

    def clear(s, _):
        head[s] = -1
        amount[s] = 0
        return 0

    lax.fori_loop(0, slot_total, clear, 0)

    def link(n, _):
        s = slots_ref[n]

        @pl.when(s >= 0)
        def _():
            following[n] = head[s]
            head[s] = n
            amount[s] = amount[s] + 1

        return 0

    lax.fori_loop(0, lanes, link, 0)

    col = lax.broadcasted_iota(jnp.int32, table.shape, 0)
    out = lax.broadcasted_iota(jnp.int32, table.shape, 1)
    table[...] = jnp.where(
        jnp.logical_and(col >= LOOK * out - 12, col <= LOOK * out + 15), 1.0, 0.0
    ).astype(table.dtype)
    up[:, rows_out:, :] = jnp.zeros((fields, 8, width), jnp.float32)
    low[:, :8, :] = jnp.zeros((fields, 8, width), jnp.float32)

    def block_row(r, _):
        for c in range(TILE_WIDE_PARTS):
            s = r * TILE_WIDE_PARTS + c
            first = head[s]
            place = slice(c * channels * side, (c + 1) * channels * side)

            @pl.when(first < 0)
            def _():
                image[place] = jnp.zeros((channels * side, side), jnp.float32)

            @pl.when(first >= 0)
            def _():
                count = jnp.full((8, side), amount[s], jnp.int32).astype(jnp.float32)
                scale = (1.0 / count)[:1]
                image[place] = arrived_ref[first].astype(jnp.float32) * scale

                def more(n):
                    image[place] += arrived_ref[n].astype(jnp.float32) * scale
                    return following[n]

                lax.while_loop(lambda n: n >= 0, more, following[first])

        def chunk(i, _):
            c = i // (looks_down // 8)
            rows = lax.rem(i, looks_down // 8) * 8
            columns = pl.ds(pl.multiple_of(c * side, side), side)
            own, above, below = None, None, None
            for phase in range(LOOK):
                values = [
                    image[pl.ds((c * channels + ch) * side + rows * LOOK + phase, 8, stride=LOOK), :]
                    for ch in range(channels)
                ]
                re, im = values[0::2], values[1::2]
                now = (
                    [re[k] * re[k + 1] + im[k] * im[k + 1] for k in range(pairs)]
                    + [im[k] * re[k + 1] - re[k] * im[k + 1] for k in range(pairs)]
                    + [re[d] * re[d] + im[d] * im[d] for d in range(dates)]
                )
                own = now if phase == 0 else [a + b for a, b in zip(own, now)]
                if phase == 1:
                    above = own
                if phase == LOOK - 1:
                    below = now
            at = r * looks_down + rows
            for f in range(fields):
                mid[f, pl.ds(pl.multiple_of(at, 8), 8), columns] = own[f]
                up[f, pl.ds(pl.multiple_of(at, 8), 8), columns] = above[f]
                low[f, pl.ds(pl.multiple_of(at + 8, 8), 8), columns] = below[f]
            return 0

        lax.fori_loop(0, TILE_WIDE_PARTS * (looks_down // 8), chunk, 0)
        return 0

    lax.fori_loop(0, TILE_TALL_PARTS, block_row, 0)

    def columns_pass(f, _):
        total = mid[f] + up[f, 1 : rows_out + 1, :] + low[f, 7 : rows_out + 7, :]
        box_ref[f] = split_dot(total, table[...])
        return 0

    lax.fori_loop(0, fields, columns_pass, 0)
    edges[...] = jnp.zeros_like(edges)
    for f in range(fields):
        edges[f : f + 1] = up[f, 0:1, :]
        edges[16 + f : 17 + f] = low[f, rows_out + 7 : rows_out + 8, :]
    edge_ref[...] = split_dot(edges[...], table[...])


def looks(slots, arrived, dates):
    lanes, rows, side = arrived.shape
    fields = 3 * dates - 2
    width = TILE_WIDE_PARTS * side
    rows_out = TILE_TALL_PARTS * side // LOOK
    cols_out = width // LOOK
    slot_total = TILE_TALL_PARTS * TILE_WIDE_PARTS
    return pl.pallas_call(
        functools.partial(looks_kernel, dates, side),
        out_shape=(
            jax.ShapeDtypeStruct((fields, rows_out, cols_out), jnp.float32),
            jax.ShapeDtypeStruct((32, cols_out), jnp.float32),
        ),
        in_specs=[
            pl.BlockSpec(memory_space=pltpu.SMEM),
            pl.BlockSpec(memory_space=pltpu.VMEM),
        ],
        out_specs=(pl.BlockSpec(memory_space=pltpu.VMEM), pl.BlockSpec(memory_space=pltpu.VMEM)),
        scratch_shapes=[
            pltpu.VMEM((TILE_WIDE_PARTS * rows, side), jnp.float32),
            pltpu.VMEM((fields, rows_out, width), jnp.float32),
            pltpu.VMEM((fields, rows_out + 8, width), jnp.float32),
            pltpu.VMEM((fields, rows_out + 8, width), jnp.float32),
            pltpu.VMEM((32, width), jnp.float32),
            pltpu.VMEM((width, cols_out), jnp.bfloat16),
            pltpu.SMEM((slot_total,), jnp.int32),
            pltpu.SMEM((lanes,), jnp.int32),
            pltpu.SMEM((slot_total,), jnp.int32),
        ],
        compiler_params=pltpu.CompilerParams(vmem_limit_bytes=58 * MIB),
    )(slots, arrived)


def local(radar_subimages, owning_sector, sector_down_start, sector_across_start):
    held, dates, parts, side, _ = radar_subimages.shape
    blocks = radar_subimages.reshape(held, dates * parts * side, side)
    arrived, notes = exchange(
        blocks, owning_sector[:, 0], sector_down_start, sector_across_start
    )
    slots = notes[:, 0, :SUBIMAGE_BOUND].reshape(-1)
    box, edge = looks(slots, arrived.reshape(-1, dates * parts * side, side), dates)
    count = lax.axis_size("grid")
    fields = box.shape[0]
    after = lax.ppermute(edge[:fields], "grid", [(i + 1, i) for i in range(count - 1)])
    before = lax.ppermute(edge[16 : 16 + fields], "grid", [(i, i + 1) for i in range(count - 1)])
    row = lax.broadcasted_iota(jnp.int32, box.shape, 1)
    box = box + jnp.where(row == 0, before[:, None, :], 0.0)
    box = box + jnp.where(row == box.shape[1] - 1, after[:, None, :], 0.0)
    pairs = dates - 1
    magnitude = jnp.sqrt(box[:pairs] ** 2 + box[pairs : 2 * pairs] ** 2)
    scale_root = jnp.sqrt(box[2 * pairs : 3 * pairs] * box[2 * pairs + 1 :] + EPSILON)
    return magnitude / scale_root


def solution(mesh):
    in_specs = (
        P(("region", "grid"), None, None, None, None),
        P(("region", "grid"), None),
        P(("region", "grid")),
        P(("region", "grid")),
    )
    out_specs = P(None, ("region", "grid"), None)
    return jax.shard_map(local, mesh=mesh, in_specs=in_specs, out_specs=out_specs, check_vma=False)
```

time: 318 us -> 226 us (0.71)
  Pallas kernels: 0 us -> 203 us
  waiting for transfers between devices: 183 us -> 1.4 us
  local copies, waits for them, and re-layouts: 59.5 us -> 9.36 us
  other arithmetic: 28.2 us -> 2.53 us
  matrix products: 25.5 us -> 0 us
  starting transfers between devices: 18.9 us -> 6.6 us
    pallas_call x0 -> x2, Pallas kernels: none -> 203 us  [the longest x1 186 us: exchange(): pl.pallas_call(functools.partial(exchange_kernel, group), out_shape=(jax....]
    all_to_all x2 -> x0, waiting for transfers between devices: 181 us -> none  [the longest x1 181 us: local(): lax.all_to_all(outgoing, 'grid', split_axis=0, concat_axis=0, tiled=True)]
    dot_general x3 -> x0, matrix products: 25.5 us -> none  [the longest x1 15.8 us: columns_pass(): jnp.einsum('frc,cj->frj', fields, window_table, precision=lax.Precision.H...]
    reshape x2 -> x0, local copies, waits for them, and re-layouts: 24 us -> none  [the longest x1 18 us: assemble(): merged_image.transpose(2, 3, 0, 4, 1, 5)]
    select_n x2 -> x0, local copies, waits for them, and re-layouts: 17 us -> none  [the longest x1 16.3 us: local(): jnp.where(used_entries[:, None, None, None, None], radar_subimages[receiv...]
    all_to_all x2 -> x0, starting transfers between devices: 12.2 us -> none  [the longest x1 6.18 us: local(): lax.all_to_all(lane_slot, 'grid', split_axis=0, concat_axis=0, tiled=True)]
    add x6 -> x1, other arithmetic: 11.8 us -> 1.6 us  [local(): box = box + jnp.where(row == box.shape[1] - 1, after[:, None, :], 0.0)]
    gather x2 -> x0, local copies, waits for them, and re-layouts: 8.46 us -> none  [the longest x1 7.76 us: local(): radar_subimages[received_entry]]
  transfers between devices with their start and end apart: 4 -> 2, of which waited for: 2 -> 1; matrix products, arithmetic and copies ran while one was open for 10% -> 0% of each run, Pallas kernels for 0% -> 0%
where the time goes in v1:
time: 226 us; the launch traced here: 223 us
  Pallas kernels  203 us (90%)
  local copies, waits for them, and re-layouts  9.36 us (4%)
  starting transfers between devices  6.6 us (3%)
  other arithmetic  2.53 us (1%)
    pallas_call x1, Pallas kernels, exchange(): pl.pallas_call(functools.partial(exchange_kernel, group), out_shape=(jax....  186 us
    pallas_call x1, Pallas kernels, looks(): pl.pallas_call(functools.partial(looks_kernel, dates, side), out_shape=(j...  16.2 us
    unnamed x10, local copies, waits for them, and re-layouts  7.97 us
    ppermute x1, starting transfers between devices, local(): lax.ppermute(edge[:fields], 'grid', [(i + 1, i) for i in range(count - 1)])  4.69 us
  transfers between devices with their start and end apart: 2, of which 1 were waited for; matrix products, arithmetic and copies ran while one was open for 0% of the time, Pallas kernels for 0%

profile of v1, /device:TPU:16, one launch (start us, length us, event | category | flops | bytes accessed | tf_op | source)
XLA Modules:
  0.0 222.6 jit_solution(16940073359924682759)
XLA Ops:
  0.0 0.0 copy-start.1
  0.0 2.8 %copy-done.1 = bf16[24,4,2,128,128]{4,3,2,1,0:T(8,128)(2,1)S(1)} copy-done((bf16[24,4,2,128,128]{4,3,2,1,0:T(8,128)(2,1)S(1)}, bf16[24,4,2,128,128]{4,3,2,1,0:T(8,128)(2,1)}, u32[]{:S(2)}) %copy-start.1) | copy-done | bytes 6291480
  2.8 0.0 copy-start.2
  2.8 0.7 copy-done.2
  3.4 0.0 copy-start.3
  3.4 0.7 copy-done.3
  4.1 0.0 copy-start.4
  4.1 0.7 copy-done.4
  4.8 186.4 %shard_map.46 = (bf16[16,2,1024,128]{3,2,1,0:T(8,128)(2,1)S(1)}, s32[16,8,128]{2,1,0:T(8,128)S(1)}) custom-call(s32[24]{0:T(128)S(1)} %bitcast.5, s32[24]{0:T(128)S(1)} %copy-done.3, s32[24]{0:T(128)S(1)} %copy-done.4, bf16[24,1024,128]{2,1,0:T(8,128)(2,1)S(1)} %bitcast.4), custom_call_target="tpu_custom_call" | custom-call | tf_op jit(solution)/shard_map/pallas_call | solution.py:120
  191.2 0.0 copy-start
  191.2 3.2 %copy-done = bf16[16,2,1024,128]{3,2,1,0:T(8,128)(2,1)} copy-done((bf16[16,2,1024,128]{3,2,1,0:T(8,128)(2,1)}, bf16[16,2,1024,128]{3,2,1,0:T(8,128)(2,1)S(1)}, u32[]{:S(2)}) %copy-start) | copy-done | bytes 8388632
  194.5 0.6 reshape_squeeze.3.slots_ref
  195.1 16.2 %shard_map.47 = (f32[10,128,256]{2,1,0:T(8,128)}, f32[32,256]{1,0:T(8,128)}) custom-call(s32[32]{0:T(128)} %reshape_squeeze.3.slots_ref, bf16[32,1024,128]{2,1,0:T(8,128)(2,1)} %bitcast.3), custom_call_target="tpu_custom_call" | custom-call | tf_op jit(solution)/shard_map/pallas_call | solution.py:272
  211.3 0.7 fusion.5
  212.0 1.9 collective-permute-start
  213.9 4.7 %collective-permute-start.1 = (f32[10,256]{1,0:T(8,128)S(1)}, f32[10,256]{1,0:T(8,128)S(1)}, u32[]{:S(2)}, u32[]{:S(2)}) collective-permute-start(f32[10,256]{1,0:T(8,128)S(1)} %get-tuple-element.14), channel_id=1, source_target_pairs={{1,0},{2,1},{3,2},{4,3},{5,4},{6,5},{7,6},{8,7},{9,8},{10,9},{11,1... | collective-permute-start | bytes 30728 | tf_op jit(solution)/shard_map/ppermute | solution.py:308
  218.6 0.0 collective-permute-done
  218.6 1.4 collective-permute-done.1
  220.0 1.6 select_add_fusion
  221.6 0.9 fusion.2
  (2 shorter events, 0.0 us)
Async XLA Ops:
  0.0 2.8 %copy-start.1 = (bf16[24,4,2,128,128]{4,3,2,1,0:T(8,128)(2,1)S(1)}, bf16[24,4,2,128,128]{4,3,2,1,0:T(8,128)(2,1)}, u32[]{:S(2)}) copy-start(bf16[24,4,2,128,128]{4,3,2,1,0:T(8,128)(2,1)} %param.4) | copy-start | bytes 18874372
  2.8 0.7 copy-start.2
  3.4 0.7 copy-start.3
  4.1 0.7 copy-start.4
  191.2 3.2 %copy-start = (bf16[16,2,1024,128]{3,2,1,0:T(8,128)(2,1)}, bf16[16,2,1024,128]{3,2,1,0:T(8,128)(2,1)S(1)}, u32[]{:S(2)}) copy-start(bf16[16,2,1024,128]{3,2,1,0:T(8,128)(2,1)S(1)} %get-tuple-element.10) | copy-start | bytes 25165828
  212.0 6.6 %collective-permute-start = (f32[10,256]{1,0:T(8,128)S(1)}, f32[10,256]{1,0:T(8,128)S(1)}, u32[]{:S(2)}, u32[]{:S(2)}) collective-permute-start(f32[10,256]{1,0:T(8,128)S(1)} %get-tuple-element.13), channel_id=1, source_target_pairs={{0,1},{1,2},{2,3},{3,4},{4,5},{5,6},{6,7},{7,8},{8,9},{9,10},{10,1... | collective-permute-start | bytes 30728 | tf_op jit(solution)/shard_map/ppermute | solution.py:309
  213.9 6.1 %collective-permute-start.1 = (f32[10,256]{1,0:T(8,128)S(1)}, f32[10,256]{1,0:T(8,128)S(1)}, u32[]{:S(2)}, u32[]{:S(2)}) collective-permute-start(f32[10,256]{1,0:T(8,128)S(1)} %get-tuple-element.14), channel_id=1, source_target_pairs={{1,0},{2,1},{3,2},{4,3},{5,4},{6,5},{7,6},{8,7},{9,8},{10,9},{11,1... | collective-permute-start | bytes 30728 | tf_op jit(solution)/shard_map/ppermute | solution.py:308

commit v2 on v0

v2 whole, which is shorter than its diff:
```python
import functools

import jax
import jax.numpy as jnp
from jax import lax
from jax.experimental import pallas as pl
from jax.experimental.pallas import tpu as pltpu
from jax.sharding import PartitionSpec as P

SUBIMAGE_BOUND = 2
TILE_TALL_PARTS = 4
TILE_WIDE_PARTS = 8
LOOK = 4
BAND = 32

EPSILON = 1e-06
MIB = 1 << 20
MESH = pl.DeviceIdType.MESH


def split_dot(values, table):
    total = None
    rest = values
    for _ in range(3):
        part = rest.astype(jnp.bfloat16)
        rest = rest - part.astype(jnp.float32)
        term = jnp.dot(part, table, preferred_element_type=jnp.float32)
        total = term if total is None else total + term
    return total


def looks_kernel(
    group,
    dates,
    owner_ref,
    down_ref,
    across_ref,
    blocks_ref,
    box_ref,
    staged,
    landed,
    notes,
    landed_notes,
    slots,
    chain,
    last,
    amount,
    sums,
    image,
    lines,
    table,
    send_sem,
    recv_sem,
    note_send_sem,
    note_recv_sem,
    own_sem,
):
    me = lax.axis_index("grid")
    held = blocks_ref.shape[0]
    side = blocks_ref.shape[-1]
    bands = side // BAND
    channels = 2 * dates
    pairs = dates - 1
    fields = 2 * pairs + dates
    lanes = group * SUBIMAGE_BOUND
    slot_total = TILE_TALL_PARTS * TILE_WIDE_PARTS
    tall = BAND // LOOK
    lane = lax.broadcasted_iota(jnp.int32, notes.shape[1:], 1)

    def stage(t):
        first, second = jnp.int32(0), jnp.int32(0)
        first_slot, second_slot = jnp.int32(-1), jnp.int32(-1)
        found = jnp.int32(0)
        for b in range(held):
            hit = owner_ref[b] == t
            slot = down_ref[b] * TILE_WIDE_PARTS + across_ref[b]
            take_first = jnp.logical_and(hit, found == 0)
            take_second = jnp.logical_and(hit, found != 0)
            first = jnp.where(take_first, b, first)
            first_slot = jnp.where(take_first, slot, first_slot)
            second = jnp.where(take_second, b, second)
            second_slot = jnp.where(take_second, slot, second_slot)
            found = jnp.where(hit, 1, found)
        staged[t, 0] = blocks_ref[first]
        staged[t, 1] = blocks_ref[second]
        notes[t] = jnp.where(lane == 0, first_slot, jnp.where(lane == 1, second_slot, -1))

    def band_of(t, q):
        return staged.at[t, :, :, pl.ds(q * BAND, BAND), :]

    def band_copy(q, k):
        t = lax.rem(me + k, group)
        return pltpu.make_async_remote_copy(
            src_ref=band_of(t, q),
            dst_ref=landed[q].at[me],
            send_sem=send_sem.at[q, k],
            recv_sem=recv_sem.at[q, k],
            device_id={"grid": t},
            device_id_type=MESH,
        )

    def note_copy(k):
        t = lax.rem(me + k, group)
        return pltpu.make_async_remote_copy(
            src_ref=notes.at[t],
            dst_ref=landed_notes.at[me],
            send_sem=note_send_sem.at[k],
            recv_sem=note_recv_sem.at[k],
            device_id={"grid": t},
            device_id_type=MESH,
        )

    barrier = pltpu.get_barrier_semaphore()

    def greet(k, _):
        pl.semaphore_signal(
            barrier, inc=1, device_id={"grid": lax.rem(me + k, group)}, device_id_type=MESH
        )
        return 0

    lax.fori_loop(1, group, greet, 0)
    pl.semaphore_wait(barrier, group - 1)

    def send_first(k, _):
        stage(lax.rem(me + k, group))
        note_copy(k).start()
        band_copy(0, k).start()
        return 0

    lax.fori_loop(1, group, send_first, 0)
    for q in range(1, bands):

        def send(k, _):
            band_copy(q, k).start()
            return 0

        lax.fori_loop(1, group, send, 0)

    stage(me)
    own = [
        pltpu.make_async_copy(band_of(me, q), landed[q].at[me], own_sem.at[q]) for q in range(bands)
    ]
    own.append(pltpu.make_async_copy(notes.at[me], landed_notes.at[me], own_sem.at[bands]))
    for copy in own:
        copy.start()

    col = lax.broadcasted_iota(jnp.int32, table.shape, 0)
    out = lax.broadcasted_iota(jnp.int32, table.shape, 1)
    table[...] = jnp.where(
        jnp.logical_and(col >= LOOK * out - 12, col <= LOOK * out + 15), 1.0, 0.0
    ).astype(table.dtype)
    sums[lanes] = jnp.zeros(sums.shape[1:], jnp.float32)

    def hear(k, _):
        note_copy(k).wait()
        return 0

    lax.fori_loop(1, group, hear, 0)
    own[bands].wait()
    to_scalars = pltpu.make_async_copy(landed_notes, slots, own_sem.at[bands + 1])
    to_scalars.start()
    to_scalars.wait()

    def link(g, _):
        for j in range(SUBIMAGE_BOUND):
            mine, n = slots[g, 0, j], g * SUBIMAGE_BOUND + j

            def look(h, found):
                for i in range(SUBIMAGE_BOUND):
                    m = h * SUBIMAGE_BOUND + i
                    hit = jnp.logical_and(slots[h, 0, i] == mine, m < n)
                    found = jnp.where(hit, m, found)
                return found

            chain[n] = lax.fori_loop(0, group, look, jnp.int32(lanes))
        return 0

    lax.fori_loop(0, group, link, 0)

    def settle(s, _):
        def look(h, carry):
            found, count = carry
            for i in range(SUBIMAGE_BOUND):
                hit = slots[h, 0, i] == s
                found = jnp.where(hit, h * SUBIMAGE_BOUND + i, found)
                count = jnp.where(hit, count + 1, count)
            return found, count

        found, count = lax.fori_loop(0, group, look, (jnp.int32(lanes), jnp.int32(0)))
        last[s] = found
        amount[s] = jnp.maximum(count, 1)
        return 0

    lax.fori_loop(0, slot_total, settle, 0)
    row = lax.broadcasted_iota(jnp.int32, (tall, side), 0)
    edge_base = fields * TILE_TALL_PARTS
    edge_groups = pl.cdiv(2 * fields, tall)
    lines[edge_base:] = jnp.zeros((TILE_TALL_PARTS * edge_groups,) + lines.shape[1:], jnp.float32)

    for q in range(bands):

        def arrive(k, _):
            band_copy(q, k).wait_recv()
            return 0

        lax.fori_loop(1, group, arrive, 0)
        own[q].wait()

        def add(g, _):
            for j in range(SUBIMAGE_BOUND):
                n = g * SUBIMAGE_BOUND + j
                block = landed[q][g, j].astype(jnp.float32).reshape(sums.shape[1:])
                sums[n] = block + sums[chain[n]]
            return 0

        lax.fori_loop(0, group, add, 0)

        def block_row(r, _):
            for c in range(TILE_WIDE_PARTS):
                s = r * TILE_WIDE_PARTS + c
                count = jnp.full((8, side), amount[s], jnp.int32).astype(jnp.float32)
                scale = (1.0 / count)[:1]
                image[c * channels * BAND : (c + 1) * channels * BAND] = sums[last[s]] * scale
            for c in range(TILE_WIDE_PARTS):
                columns = slice(c * side, (c + 1) * side)
                own_sum, above, below = None, None, None
                for phase in range(LOOK):
                    values = [
                        image[pl.ds((c * channels + ch) * BAND + phase, tall, stride=LOOK), :]
                        for ch in range(channels)
                    ]
                    re, im = values[0::2], values[1::2]
                    now = (
                        [re[k] * re[k + 1] + im[k] * im[k + 1] for k in range(pairs)]
                        + [im[k] * re[k + 1] - re[k] * im[k + 1] for k in range(pairs)]
                        + [re[d] * re[d] + im[d] * im[d] for d in range(dates)]
                    )
                    own_sum = now if phase == 0 else [a + b for a, b in zip(own_sum, now)]
                    if phase == 1:
                        above = own_sum
                    if phase == LOOK - 1:
                        below = now
                for f in range(fields):
                    lines[f * TILE_TALL_PARTS + r, :, columns] = (
                        own_sum[f]
                        + jnp.where(row < tall - 1, pltpu.roll(above[f], tall - 1, 0), 0.0)
                        + jnp.where(row > 0, pltpu.roll(below[f], 1, 0), 0.0)
                    )
                    edge = edge_base + r * edge_groups
                    e = fields + f
                    lines[edge + f // tall, f % tall : f % tall + 1, columns] = above[f][:1]
                    lines[edge + e // tall, e % tall : e % tall + 1, columns] = below[f][tall - 1 :]
            return 0

        lax.fori_loop(0, TILE_TALL_PARTS, block_row, 0)
        box_ref[q] = split_dot(lines[...].reshape(-1, lines.shape[-1]), table[...])

    for q in range(bands):

        def sent(k, _):
            band_copy(q, k).wait_send()
            return 0

        lax.fori_loop(1, group, sent, 0)


def looks(blocks, owner, down, across):
    group = lax.axis_size("grid")
    held, channels, side, _ = blocks.shape
    dates = channels // 2
    lanes = group * SUBIMAGE_BOUND
    bands = side // BAND
    slot_total = TILE_TALL_PARTS * TILE_WIDE_PARTS
    fields = 3 * dates - 2
    width = TILE_WIDE_PARTS * side
    tall = BAND // LOOK
    groups = TILE_TALL_PARTS * (fields + pl.cdiv(2 * fields, tall))
    return pl.pallas_call(
        functools.partial(looks_kernel, group, dates),
        out_shape=jax.ShapeDtypeStruct((bands, groups * tall, width // LOOK), jnp.float32),
        in_specs=[pl.BlockSpec(memory_space=pltpu.SMEM)] * 3
        + [pl.BlockSpec(memory_space=pltpu.VMEM)],
        out_specs=pl.BlockSpec(memory_space=pltpu.VMEM),
        scratch_shapes=[
            pltpu.VMEM((group, SUBIMAGE_BOUND, channels, side, side), blocks.dtype),
            tuple(
                pltpu.VMEM((group, SUBIMAGE_BOUND, channels, BAND, side), blocks.dtype)
                for _ in range(bands)
            ),
            pltpu.VMEM((group, 8, side), jnp.int32),
            pltpu.VMEM((group, 8, side), jnp.int32),
            pltpu.SMEM((group, 8, side), jnp.int32),
            pltpu.SMEM((lanes,), jnp.int32),
            pltpu.SMEM((slot_total,), jnp.int32),
            pltpu.SMEM((slot_total,), jnp.int32),
            pltpu.VMEM((lanes + 1, channels * BAND, side), jnp.float32),
            pltpu.VMEM((TILE_WIDE_PARTS * channels * BAND, side), jnp.float32),
            pltpu.VMEM((groups, tall, width), jnp.float32),
            pltpu.VMEM((width, width // LOOK), jnp.bfloat16),
            pltpu.SemaphoreType.DMA((bands, group)),
            pltpu.SemaphoreType.DMA((bands, group)),
            pltpu.SemaphoreType.DMA((group,)),
            pltpu.SemaphoreType.DMA((group,)),
            pltpu.SemaphoreType.DMA((bands + 2,)),
        ],
        compiler_params=pltpu.CompilerParams(
            collective_id=0, has_side_effects=True, vmem_limit_bytes=60 * MIB
        ),
    )(owner, down, across, blocks)


def local(radar_subimages, owning_sector, sector_down_start, sector_across_start):
    held, dates, parts, side, _ = radar_subimages.shape
    blocks = radar_subimages.reshape(held, dates * parts, side, side)
    box = looks(blocks, owning_sector[:, 0], sector_down_start, sector_across_start)
    count = lax.axis_size("grid")
    bands, _, cols = box.shape
    pairs = dates - 1
    fields = 2 * pairs + dates
    tall = BAND // LOOK
    steps = TILE_TALL_PARTS * bands
    edge_base = fields * TILE_TALL_PARTS * tall
    edges = box[:, edge_base:].reshape(bands, TILE_TALL_PARTS, -1, cols)[:, :, : 2 * fields]
    edges = edges.transpose(2, 1, 0, 3).reshape(2 * fields, steps, cols)
    above, below = edges[:fields], edges[fields:]
    after = lax.ppermute(above[:, 0], "grid", [(i + 1, i) for i in range(count - 1)])
    before = lax.ppermute(below[:, -1], "grid", [(i, i + 1) for i in range(count - 1)])
    above = jnp.concatenate([above[:, 1:], after[:, None]], 1)[:, :, None]
    below = jnp.concatenate([before[:, None], below[:, :-1]], 1)[:, :, None]
    box = box[:, :edge_base].reshape(bands, fields, TILE_TALL_PARTS, tall, cols)
    box = box.transpose(1, 2, 0, 3, 4).reshape(fields, steps, tall, cols)
    row = lax.broadcasted_iota(jnp.int32, box.shape, 2)
    box = box + jnp.where(row == tall - 1, above, 0.0) + jnp.where(row == 0, below, 0.0)
    magnitude = jnp.sqrt(box[:pairs] ** 2 + box[pairs : 2 * pairs] ** 2)
    scale_root = jnp.sqrt(box[2 * pairs : 3 * pairs] * box[2 * pairs + 1 :] + EPSILON)
    return (magnitude / scale_root).reshape(pairs, steps * tall, cols)


def solution(mesh):
    in_specs = (
        P(("region", "grid"), None, None, None, None),
        P(("region", "grid"), None),
        P(("region", "grid")),
        P(("region", "grid")),
    )
    out_specs = P(None, ("region", "grid"), None)
    return jax.shard_map(local, mesh=mesh, in_specs=in_specs, out_specs=out_specs, check_vma=False)
```

time: 318 us -> 208 us (0.65)
  Pallas kernels: 0 us -> 191 us
  waiting for transfers between devices: 183 us -> 2.47 us
  local copies, waits for them, and re-layouts: 59.5 us -> 2.89 us
  other arithmetic: 28.2 us -> 1.31 us
  matrix products: 25.5 us -> 0 us
  starting transfers between devices: 18.9 us -> 10.2 us
    pallas_call x0 -> x1, Pallas kernels: none -> 191 us  [looks(): pl.pallas_call(functools.partial(looks_kernel, group, dates), out_shape=j...]
    all_to_all x2 -> x0, waiting for transfers between devices: 181 us -> none  [the longest x1 181 us: local(): lax.all_to_all(outgoing, 'grid', split_axis=0, concat_axis=0, tiled=True)]
    dot_general x3 -> x0, matrix products: 25.5 us -> none  [the longest x1 15.8 us: columns_pass(): jnp.einsum('frc,cj->frj', fields, window_table, precision=lax.Precision.H...]
    reshape x2 -> x1, local copies, waits for them, and re-layouts: 24 us -> 0.14 us  [local(): box = box[:, :edge_base].reshape(bands, fields, TILE_TALL_PARTS, tall, cols)]
    select_n x2 -> x0, local copies, waits for them, and re-layouts: 17 us -> none  [the longest x1 16.3 us: local(): jnp.where(used_entries[:, None, None, None, None], radar_subimages[receiv...]
    all_to_all x2 -> x0, starting transfers between devices: 12.2 us -> none  [the longest x1 6.18 us: local(): lax.all_to_all(lane_slot, 'grid', split_axis=0, concat_axis=0, tiled=True)]
    add x6 -> x1, other arithmetic: 11.8 us -> 0.32 us  [local(): box + jnp.where(row == tall - 1, above, 0.0)]
    gather x2 -> x0, local copies, waits for them, and re-layouts: 8.46 us -> none  [the longest x1 7.76 us: local(): radar_subimages[received_entry]]
  transfers between devices with their start and end apart: 4 -> 2, of which waited for: 2 -> 1; matrix products, arithmetic and copies ran while one was open for 10% -> 0% of each run, Pallas kernels for 0% -> 0%
where the time goes in v2:
time: 208 us
  Pallas kernels  191 us (92%)
  starting transfers between devices  10.2 us (5%)
  local copies, waits for them, and re-layouts  2.89 us (1%)
  waiting for transfers between devices  2.47 us (1%)
    pallas_call x1, Pallas kernels, looks(): pl.pallas_call(functools.partial(looks_kernel, group, dates), out_shape=j...  191 us
    ppermute x1, starting transfers between devices, local(): lax.ppermute(above[:, 0], 'grid', [(i + 1, i) for i in range(count - 1)])  8.33 us
  transfers between devices with their start and end apart: 2, of which 1 were waited for; matrix products, arithmetic and copies ran while one was open for 0% of the time, Pallas kernels for 0%

profile of v2, /device:TPU:16, one launch (start us, length us, event | category | flops | bytes accessed | tf_op | source)
XLA Modules:
  0.0 208.0 jit_solution(7256193009017036805)
XLA Ops:
  0.0 190.9 %shard_map.46 = f32[4,416,256]{2,1,0:T(8,128)} custom-call(s32[24]{0:T(128)} %bitcast.30, s32[24]{0:T(128)} %down_ref.1, s32[24]{0:T(128)} %across_ref.1, bf16[24,8,128,128]{3,2,1,0:T(8,128)(2,1)} %bitcast.22), custom_call_target="tpu_custom_call" | custom-call | tf_op jit(solution)/shard_map/pallas_call | solution.py:278
  190.9 1.0 slice.46
  191.9 0.2 copy.17
  192.2 0.1 slice.49
  192.3 8.3 %collective-permute-start = (f32[10,256]{1,0:T(8,128)S(1)}, f32[10,256]{1,0:T(8,128)S(1)}, u32[]{:S(2)}, u32[]{:S(2)}) collective-permute-start(f32[10,256]{1,0:T(8,128)S(1)} %bitcast.27), channel_id=1, source_target_pairs={{1,0},{2,1},{3,2},{4,3},{5,4},{6,5},{7,6},{8,7},{9,8},{10,9},{11,1... | collective-permute-start | bytes 30728 | tf_op jit(solution)/shard_map/ppermute | solution.py:326
  200.6 0.1 slice.53
  200.7 1.9 collective-permute-start.1
  202.7 0.0 slice-start
  202.7 1.3 slice-done
  204.0 0.1 copy.7
  204.2 0.0 collective-permute-done
  204.2 2.5 %collective-permute-done.1 = f32[10,256]{1,0:T(8,128)S(1)} collective-permute-done((f32[10,256]{1,0:T(8,128)S(1)}, f32[10,256]{1,0:T(8,128)S(1)}, u32[]{:S(2)}, u32[]{:S(2)}) %collective-permute-start.1) | collective-permute-done | bytes 10272 | tf_op jit(solution)/shard_map/ppermute | solution.py:327
  206.7 0.3 select_add_fusion
  207.1 0.9 fusion.3
  (11 shorter events, 0.1 us)
Async XLA Ops:
  192.3 11.9 %collective-permute-start = (f32[10,256]{1,0:T(8,128)S(1)}, f32[10,256]{1,0:T(8,128)S(1)}, u32[]{:S(2)}, u32[]{:S(2)}) collective-permute-start(f32[10,256]{1,0:T(8,128)S(1)} %bitcast.27), channel_id=1, source_target_pairs={{1,0},{2,1},{3,2},{4,3},{5,4},{6,5},{7,6},{8,7},{9,8},{10,9},{11,1... | collective-permute-start | bytes 30728 | tf_op jit(solution)/shard_map/ppermute | solution.py:326
  200.7 6.0 %collective-permute-start.1 = (f32[10,256]{1,0:T(8,128)S(1)}, f32[10,256]{1,0:T(8,128)S(1)}, u32[]{:S(2)}, u32[]{:S(2)}) collective-permute-start(f32[10,256]{1,0:T(8,128)S(1)} %bitcast.29), channel_id=1, source_target_pairs={{0,1},{1,2},{2,3},{3,4},{4,5},{5,6},{6,7},{7,8},{8,9},{9,10},{10,1... | collective-permute-start | bytes 30728 | tf_op jit(solution)/shard_map/ppermute | solution.py:327
  202.7 1.3 slice-start

commit v3 on v2

--- a/solution.py
+++ b/solution.py
@@ -35,8 +35,9 @@
     owner_ref,
     down_ref,
     across_ref,
+    source_ref,
+    box_ref,
     blocks_ref,
-    box_ref,
     staged,
     landed,
     notes,
@@ -110,6 +111,8 @@
             device_id_type=MESH,
         )
 
+    fetch = pltpu.make_async_copy(source_ref, blocks_ref, own_sem.at[bands + 2])
+    fetch.start()
     barrier = pltpu.get_barrier_semaphore()
 
     def greet(k, _):
@@ -120,6 +123,7 @@
 
     lax.fori_loop(1, group, greet, 0)
     pl.semaphore_wait(barrier, group - 1)
+    fetch.wait()
 
     def send_first(k, _):
         stage(lax.rem(me + k, group))
@@ -161,14 +165,17 @@
     to_scalars.start()
     to_scalars.wait()
 
+    def sender(k):
+        return lax.rem(me + group - k, group)
+
     def link(g, _):
         for j in range(SUBIMAGE_BOUND):
-            mine, n = slots[g, 0, j], g * SUBIMAGE_BOUND + j
+            mine, n = slots[sender(g), 0, j], g * SUBIMAGE_BOUND + j
 
             def look(h, found):
                 for i in range(SUBIMAGE_BOUND):
                     m = h * SUBIMAGE_BOUND + i
-                    hit = jnp.logical_and(slots[h, 0, i] == mine, m < n)
+                    hit = jnp.logical_and(slots[sender(h), 0, i] == mine, m < n)
                     found = jnp.where(hit, m, found)
                 return found
 
@@ -181,7 +188,7 @@
         def look(h, carry):
             found, count = carry
             for i in range(SUBIMAGE_BOUND):
-                hit = slots[h, 0, i] == s
+                hit = slots[sender(h), 0, i] == s
                 found = jnp.where(hit, h * SUBIMAGE_BOUND + i, found)
                 count = jnp.where(hit, count + 1, count)
             return found, count
@@ -199,21 +206,20 @@
 
     for q in range(bands):
 
+        def add(k):
+            for j in range(SUBIMAGE_BOUND):
+                n = k * SUBIMAGE_BOUND + j
+                block = landed[q][sender(k), j].astype(jnp.float32).reshape(sums.shape[1:])
+                sums[n] = block + sums[chain[n]]
+
         def arrive(k, _):
             band_copy(q, k).wait_recv()
+            add(k)
             return 0
 
+        own[q].wait()
+        add(0)
         lax.fori_loop(1, group, arrive, 0)
-        own[q].wait()
-
-        def add(g, _):
-            for j in range(SUBIMAGE_BOUND):
-                n = g * SUBIMAGE_BOUND + j
-                block = landed[q][g, j].astype(jnp.float32).reshape(sums.shape[1:])
-                sums[n] = block + sums[chain[n]]
-            return 0
-
-        lax.fori_loop(0, group, add, 0)
 
         def block_row(r, _):
             for c in range(TILE_WIDE_PARTS):
@@ -279,9 +285,10 @@
         functools.partial(looks_kernel, group, dates),
         out_shape=jax.ShapeDtypeStruct((bands, groups * tall, width // LOOK), jnp.float32),
         in_specs=[pl.BlockSpec(memory_space=pltpu.SMEM)] * 3
-        + [pl.BlockSpec(memory_space=pltpu.VMEM)],
+        + [pl.BlockSpec(memory_space=pl.ANY)],
         out_specs=pl.BlockSpec(memory_space=pltpu.VMEM),
         scratch_shapes=[
+            pltpu.VMEM(blocks.shape, blocks.dtype),
             pltpu.VMEM((group, SUBIMAGE_BOUND, channels, side, side), blocks.dtype),
             tuple(
                 pltpu.VMEM((group, SUBIMAGE_BOUND, channels, BAND, side), blocks.dtype)
@@ -301,7 +308,7 @@
             pltpu.SemaphoreType.DMA((bands, group)),
             pltpu.SemaphoreType.DMA((group,)),
             pltpu.SemaphoreType.DMA((group,)),
-            pltpu.SemaphoreType.DMA((bands + 2,)),
+            pltpu.SemaphoreType.DMA((bands + 3,)),
         ],
         compiler_params=pltpu.CompilerParams(
             collective_id=0, has_side_effects=True, vmem_limit_bytes=60 * MIB

time: 208 us -> 206 us (level)
  no operation moved by 1% of the time
where the time goes in v3:
time: 206 us
  Pallas kernels  189 us (92%)
  starting transfers between devices  9.75 us (5%)
  local copies, waits for them, and re-layouts  2.89 us (1%)
  waiting for transfers between devices  2.47 us (1%)
    pallas_call x1, Pallas kernels, looks(): pl.pallas_call(functools.partial(looks_kernel, group, dates), out_shape=j...  189 us
    ppermute x1, starting transfers between devices, local(): lax.ppermute(above[:, 0], 'grid', [(i + 1, i) for i in range(count - 1)])  7.83 us
  transfers between devices with their start and end apart: 2, of which 1 were waited for; matrix products, arithmetic and copies ran while one was open for 0% of the time, Pallas kernels for 0%

profile of v3, /device:TPU:16, one launch (start us, length us, event | category | flops | bytes accessed | tf_op | source)
XLA Modules:
  0.0 206.1 jit_solution(16982488058670291278)
XLA Ops:
  0.0 189.5 %shard_map.46 = f32[4,416,256]{2,1,0:T(8,128)} custom-call(s32[24]{0:T(128)} %bitcast.30, s32[24]{0:T(128)} %down_ref.1, s32[24]{0:T(128)} %across_ref.1, bf16[24,8,128,128]{3,2,1,0:T(8,128)(2,1)} %bitcast.22), custom_call_target="tpu_custom_call" | custom-call | tf_op jit(solution)/shard_map/pallas_call | solution.py:284
  189.5 1.0 slice.46
  190.5 0.2 copy.17
  190.8 0.1 slice.49
  190.9 7.8 %collective-permute-start = (f32[10,256]{1,0:T(8,128)S(1)}, f32[10,256]{1,0:T(8,128)S(1)}, u32[]{:S(2)}, u32[]{:S(2)}) collective-permute-start(f32[10,256]{1,0:T(8,128)S(1)} %bitcast.27), channel_id=1, source_target_pairs={{1,0},{2,1},{3,2},{4,3},{5,4},{6,5},{7,6},{8,7},{9,8},{10,9},{11,1... | collective-permute-start | bytes 30728 | tf_op jit(solution)/shard_map/ppermute | solution.py:333
  198.7 0.1 slice.53
  198.8 1.9 collective-permute-start.1
  200.8 0.0 slice-start
  200.8 1.3 slice-done
  202.1 0.1 copy.7
  202.2 0.0 collective-permute-done
  202.3 2.5 %collective-permute-done.1 = f32[10,256]{1,0:T(8,128)S(1)} collective-permute-done((f32[10,256]{1,0:T(8,128)S(1)}, f32[10,256]{1,0:T(8,128)S(1)}, u32[]{:S(2)}, u32[]{:S(2)}) %collective-permute-start.1) | collective-permute-done | bytes 10272 | tf_op jit(solution)/shard_map/ppermute | solution.py:334
  204.8 0.3 select_add_fusion
  205.1 0.9 fusion.3
  (11 shorter events, 0.1 us)
Async XLA Ops:
  190.9 11.4 %collective-permute-start = (f32[10,256]{1,0:T(8,128)S(1)}, f32[10,256]{1,0:T(8,128)S(1)}, u32[]{:S(2)}, u32[]{:S(2)}) collective-permute-start(f32[10,256]{1,0:T(8,128)S(1)} %bitcast.27), channel_id=1, source_target_pairs={{1,0},{2,1},{3,2},{4,3},{5,4},{6,5},{7,6},{8,7},{9,8},{10,9},{11,1... | collective-permute-start | bytes 30728 | tf_op jit(solution)/shard_map/ppermute | solution.py:333
  198.8 6.0 %collective-permute-start.1 = (f32[10,256]{1,0:T(8,128)S(1)}, f32[10,256]{1,0:T(8,128)S(1)}, u32[]{:S(2)}, u32[]{:S(2)}) collective-permute-start(f32[10,256]{1,0:T(8,128)S(1)} %bitcast.29), channel_id=1, source_target_pairs={{0,1},{1,2},{2,3},{3,4},{4,5},{5,6},{6,7},{7,8},{8,9},{9,10},{10,1... | collective-permute-start | bytes 30728 | tf_op jit(solution)/shard_map/ppermute | solution.py:334
  200.8 1.3 slice-start

commit v4 on v3

--- a/solution.py
+++ b/solution.py
@@ -21,7 +21,7 @@
 def split_dot(values, table):
     total = None
     rest = values
-    for _ in range(3):
+    for _ in range(2):
         part = rest.astype(jnp.bfloat16)
         rest = rest - part.astype(jnp.float32)
         term = jnp.dot(part, table, preferred_element_type=jnp.float32)

time: 206 us -> 206 us (level)
  no operation moved by 1% of the time
where the time goes in v4:
time: 206 us
  Pallas kernels  189 us (92%)
  starting transfers between devices  9.32 us (5%)
  local copies, waits for them, and re-layouts  2.89 us (1%)
  waiting for transfers between devices  2.47 us (1%)
    pallas_call x1, Pallas kernels, looks(): pl.pallas_call(functools.partial(looks_kernel, group, dates), out_shape=j...  189 us
    ppermute x1, starting transfers between devices, local(): lax.ppermute(above[:, 0], 'grid', [(i + 1, i) for i in range(count - 1)])  7.4 us
  transfers between devices with their start and end apart: 2, of which 1 were waited for; matrix products, arithmetic and copies ran while one was open for 0% of the time, Pallas kernels for 0%

profile of v4, /device:TPU:16, one launch (start us, length us, event | category | flops | bytes accessed | tf_op | source)
XLA Modules:
  0.0 205.6 jit_solution(17491755007415511616)
XLA Ops:
  0.0 189.5 %shard_map.46 = f32[4,416,256]{2,1,0:T(8,128)} custom-call(s32[24]{0:T(128)} %bitcast.30, s32[24]{0:T(128)} %down_ref.1, s32[24]{0:T(128)} %across_ref.1, bf16[24,8,128,128]{3,2,1,0:T(8,128)(2,1)} %bitcast.22), custom_call_target="tpu_custom_call" | custom-call | tf_op jit(solution)/shard_map/pallas_call | solution.py:284
  189.5 1.0 slice.46
  190.5 0.2 copy.17
  190.8 0.1 slice.49
  190.9 7.4 %collective-permute-start = (f32[10,256]{1,0:T(8,128)S(1)}, f32[10,256]{1,0:T(8,128)S(1)}, u32[]{:S(2)}, u32[]{:S(2)}) collective-permute-start(f32[10,256]{1,0:T(8,128)S(1)} %bitcast.27), channel_id=1, source_target_pairs={{1,0},{2,1},{3,2},{4,3},{5,4},{6,5},{7,6},{8,7},{9,8},{10,9},{11,1... | collective-permute-start | bytes 30728 | tf_op jit(solution)/shard_map/ppermute | solution.py:333
  198.3 0.1 slice.53
  198.4 1.9 collective-permute-start.1
  200.3 0.0 slice-start
  200.3 1.3 slice-done
  201.6 0.1 copy.7
  201.8 0.0 collective-permute-done
  201.9 2.5 %collective-permute-done.1 = f32[10,256]{1,0:T(8,128)S(1)} collective-permute-done((f32[10,256]{1,0:T(8,128)S(1)}, f32[10,256]{1,0:T(8,128)S(1)}, u32[]{:S(2)}, u32[]{:S(2)}) %collective-permute-start.1) | collective-permute-done | bytes 10272 | tf_op jit(solution)/shard_map/ppermute | solution.py:334
  204.4 0.3 select_add_fusion
  204.7 0.9 fusion.3
  (11 shorter events, 0.1 us)
Async XLA Ops:
  190.9 10.9 %collective-permute-start = (f32[10,256]{1,0:T(8,128)S(1)}, f32[10,256]{1,0:T(8,128)S(1)}, u32[]{:S(2)}, u32[]{:S(2)}) collective-permute-start(f32[10,256]{1,0:T(8,128)S(1)} %bitcast.27), channel_id=1, source_target_pairs={{1,0},{2,1},{3,2},{4,3},{5,4},{6,5},{7,6},{8,7},{9,8},{10,9},{11,1... | collective-permute-start | bytes 30728 | tf_op jit(solution)/shard_map/ppermute | solution.py:333
  198.4 6.0 %collective-permute-start.1 = (f32[10,256]{1,0:T(8,128)S(1)}, f32[10,256]{1,0:T(8,128)S(1)}, u32[]{:S(2)}, u32[]{:S(2)}) collective-permute-start(f32[10,256]{1,0:T(8,128)S(1)} %bitcast.29), channel_id=1, source_target_pairs={{0,1},{1,2},{2,3},{3,4},{4,5},{5,6},{6,7},{7,8},{8,9},{9,10},{10,1... | collective-permute-start | bytes 30728 | tf_op jit(solution)/shard_map/ppermute | solution.py:334
  200.3 1.3 slice-start
